TPU v7x, 256 devices: a whole 4x4x8 slice. The times are simulated.
256 devices in a mesh: rows: 16 (over y, z_lo), pairs: 16 (over x, z_hi, core).
Axes of the slice: x: 4, y: 4, z: 8 (z_hi: 2, z_lo: 4; z = z_hi * 4 + z_lo), core: 2. Of those that a mesh axis runs over, the one named last changes fastest.
Arguments:
- snapshots: float32 [8192, 8192], P('rows', 'pairs')
- pairing: int32 [5, 16, 8], P(None, 'pairs'), may hold values from 0 to 7, each once within a row
Outputs:
- rotated: float32 [8192, 8192], P('rows', 'pairs')
Inputs may be any that keep to these rules, and one draw needn't show every extreme that they name: Each row pairing[r, g, :] is a permutation of the slots 0 .. 7.
All inputs are finite; a program needn't handle non-finite values. Where the computation divides by a largest or mean magnitude, that divisor is 1e-20 or more.
Results may differ from a plain program's by a relative error of at most 0.00024.
Values sent between devices are 32-bit elements; how exact they have to be, the bound alone decides.
No kernel may reach another device: no remote copies, remote signals or barrier semaphores. Data moves between devices by JAX's collectives and lax.ppermute only.
A program may use at most 64 MiB of HBM per device.

v0:
```python
import functools

import jax
import jax.numpy as jnp
from jax import lax
from jax.experimental import pallas as pl
from jax.experimental.pallas import tpu as pltpu
from jax.sharding import PartitionSpec as P

BLK = 64
WIDE = 2 * BLK
ROUNDS = 5
NS_STEPS = 6

VMEM = pl.BlockSpec(memory_space=pltpu.VMEM)
SMEM = pl.BlockSpec(memory_space=pltpu.SMEM)


def halves(x):
    high = x.astype(jnp.bfloat16)
    low = (x - high.astype(jnp.float32)).astype(jnp.bfloat16)
    return high, low


def left_form(x):
    return jnp.concatenate(halves(x), axis=1)


def right_form(x):
    row = jnp.concatenate(halves(x), axis=1)
    return jnp.concatenate([row, row], axis=0)


def folded(left, right):
    out = jnp.dot(left, right, preferred_element_type=jnp.float32)
    half = out.shape[1] // 2
    return out[:, :half] + out[:, half:]


def joined(k, high_ref, low_ref):
    both = slice(2 * k, 2 * k + 2)
    rows = high_ref.shape[2]
    return jnp.concatenate(
        [high_ref[both].reshape(WIDE, rows), low_ref[both].reshape(WIDE, rows)], axis=0
    )


def times(turn, both):
    high, low = halves(turn)
    left = jnp.concatenate(
        [jnp.concatenate([high, high], axis=1), jnp.concatenate([low, low], axis=1)], axis=0
    )
    out = jnp.dot(left, both, preferred_element_type=jnp.float32)
    return out[:BLK] + out[BLK:]


def places():
    row = lax.broadcasted_iota(jnp.int32, (BLK, WIDE), 0)
    lane = lax.broadcasted_iota(jnp.int32, (BLK, WIDE), 1)
    return row, lane


def packed(gram):
    row, lane = places()
    top, bottom = gram[:BLK], gram[BLK:]
    diag = jnp.sum(jnp.where(row == lane, top, 0.0), axis=0, keepdims=True) + jnp.sum(
        jnp.where(row + BLK == lane, bottom, 0.0), axis=0, keepdims=True
    )
    return jnp.where(row > lane, pltpu.roll(bottom, BLK, 1), top), diag


def unpacked(main, diag):
    row, lane = places()
    flipped = main.T
    flipped = jnp.concatenate([flipped[:BLK], flipped[BLK:]], axis=1)
    top = jnp.where(row > lane, flipped, main)
    under = (lane >= BLK) & (row + BLK > lane)
    bottom = jnp.where(under, pltpu.roll(main, BLK, 1), pltpu.roll(flipped, BLK, 1))
    bottom = jnp.where(row + BLK == lane, diag, bottom)
    return jnp.concatenate([top, bottom], axis=0)


def write_grams(high_ref, low_ref, sums_ref):
    count = high_ref.shape[0] // 2
    sums_ref[count * BLK :] = jnp.zeros_like(sums_ref[count * BLK :])
    for k in range(count):
        both = joined(k, high_ref, low_ref)
        out = lax.dot_general(
            both[:WIDE], both, (((1,), (1,)), ((), ())), preferred_element_type=jnp.float32
        )
        cross = out[:, WIDE:]
        main, diag = packed(out[:, :WIDE] + (cross + cross.T))
        sums_ref[k * BLK : (k + 1) * BLK] = main
        sums_ref[count * BLK + k : count * BLK + k + 1] = diag


def seats(step, order_ref, seat_ref):
    for place in range(order_ref.shape[2]):
        seat_ref[order_ref[step, 0, place]] = place


def open_kernel(order_ref, block_ref, high_ref, low_ref, sums_ref, seat_ref):
    seats(0, order_ref, seat_ref)
    turned_block = block_ref[...].T
    for slot in range(high_ref.shape[0]):
        seat = seat_ref[slot]
        high_ref[seat], low_ref[seat] = halves(turned_block[slot * BLK : (slot + 1) * BLK])
    write_grams(high_ref, low_ref, sums_ref)


def gram_kernel(
    step, order_ref, kept_high, kept_low, arrived_ref, high_ref, low_ref, sums_ref, seat_ref
):
    seats(step, order_ref, seat_ref)
    for k in range(arrived_ref.shape[0]):
        seat = seat_ref[2 * k]
        high_ref[seat], low_ref[seat] = kept_high[k], kept_low[k]
        seat = seat_ref[2 * k + 1]
        high_ref[seat], low_ref[seat] = halves(arrived_ref[k])
    write_grams(high_ref, low_ref, sums_ref)


def four(a, b, c, d):
    return (a + b) + (c + d)


def turned(gram):
    row = lax.broadcasted_iota(jnp.int32, (WIDE, WIDE), 0)
    col = lax.broadcasted_iota(jnp.int32, (WIDE, WIDE), 1)
    on_diag = row == col
    eye = on_diag.astype(jnp.float32)
    ymats, zmats, outer = [], [], []
    for g in gram:
        only = jnp.where(on_diag, g, 0.0)
        diag_col = jnp.sum(only, axis=1, keepdims=True) + 1e-06
        diag_row = jnp.sum(only, axis=0, keepdims=True) + 1e-06
        scale_row = lax.rsqrt(diag_row)
        unit = g * lax.rsqrt(diag_col) * scale_row
        bound = jnp.max(jnp.sum(jnp.abs(unit), axis=1, keepdims=True), axis=0, keepdims=True)
        ymats.append(unit / bound)
        outer.append((jnp.sqrt(diag_col) * lax.rsqrt(bound), scale_row))
    for step in range(NS_STEPS):
        if step == 0:
            prods = [1.5 * eye - 0.5 * y for y in ymats]
            ymats = [folded(left_form(y), right_form(p)) for y, p in zip(ymats, prods)]
            zmats = prods
            continue
        prods = [
            1.5 * eye - 0.5 * folded(left_form(z), right_form(y)) for z, y in zip(zmats, ymats)
        ]
        if step == NS_STEPS - 1:
            zmats = [folded(left_form(z), right_form(p)) for z, p in zip(zmats, prods)]
        else:
            news = [
                folded(left_form(jnp.concatenate([y, z], axis=0)), right_form(p))
                for y, z, p in zip(ymats, zmats, prods)
            ]
            ymats = [new[:WIDE] for new in news]
            zmats = [new[WIDE:] for new in news]
    return [z * a * b for z, (a, b) in zip(zmats, outer)]


def move_kernel(high_ref, low_ref, sums_ref, move_ref, first_ref):
    count = move_ref.shape[0]
    grams = [
        unpacked(
            sums_ref[k * BLK : (k + 1) * BLK], sums_ref[count * BLK + k : count * BLK + k + 1]
        )
        for k in range(count)
    ]
    for k, turn in enumerate(turned(grams)):
        first_ref[k] = turn[:BLK]
        move_ref[k] = times(turn[BLK:], joined(k, high_ref, low_ref))


def stay_kernel(high_ref, low_ref, first_ref, kept_high, kept_low):
    for k in range(first_ref.shape[0]):
        kept_high[k], kept_low[k] = halves(times(first_ref[k], joined(k, high_ref, low_ref)))


def last_stay_kernel(high_ref, low_ref, first_ref, kept_ref):
    for k in range(first_ref.shape[0]):
        kept_ref[k] = times(first_ref[k], joined(k, high_ref, low_ref))


def close_kernel(kept_ref, arrived_ref, out_ref):
    for k in range(kept_ref.shape[0]):
        pair = jnp.concatenate([kept_ref[k], arrived_ref[k]], axis=0)
        out_ref[:, k * WIDE : (k + 1) * WIDE] = pair.T


def call(kernel, shapes, *operands, scratch=()):
    return pl.pallas_call(
        kernel,
        out_shape=shapes,
        in_specs=[SMEM if x.dtype == jnp.int32 else VMEM for x in operands],
        out_specs=jax.tree.map(lambda _: VMEM, shapes),
        scratch_shapes=scratch,
    )(*operands)


def along_y(r, d):
    return (r // 4 ^ d) * 4 + r % 4


def along_z(r, d):
    return r ^ d


def from_four(value, other):
    rows = range(lax.axis_size("rows"))
    return [value] + [
        lax.ppermute(value, "rows", [(r, other(r, d)) for r in rows]) for d in (1, 2, 3)
    ]


def body(snapshots, pairing):
    rows, columns = snapshots.shape
    slots = pairing.shape[2]
    count = slots // 2
    ring = lax.axis_size("pairs")
    along = [(source, (source + 1) % ring) for source in range(ring)]

    def of(dtype, *shape):
        return jax.ShapeDtypeStruct(shape, dtype)

    split = (of(jnp.bfloat16, slots, BLK, rows),) * 2
    half = of(jnp.float32, count, BLK, rows)
    half_split = (of(jnp.bfloat16, count, BLK, rows),) * 2
    sums = of(jnp.float32, count * BLK + 8, WIDE)
    turn = of(jnp.float32, count, BLK, WIDE)

    seat = [pltpu.SMEM((slots,), jnp.int32)]
    high, low, gram = call(open_kernel, (*split, sums), pairing, snapshots, scratch=seat)
    for step in range(ROUNDS):
        part = four(*from_four(gram, along_y))
        total = four(*from_four(part, along_z))
        move, first = call(move_kernel, (half, turn), high, low, total)
        arrived = lax.ppermute(move, "pairs", along)
        if step == ROUNDS - 1:
            kept = call(last_stay_kernel, half, high, low, first)
            return call(close_kernel, of(jnp.float32, rows, columns), kept, arrived)
        kept = call(stay_kernel, half_split, high, low, first)
        high, low, gram = call(
            functools.partial(gram_kernel, step + 1),
            (*split, sums),
            pairing,
            *kept,
            arrived,
            scratch=seat,
        )


def solution(mesh):
    placed = (P("rows", "pairs"), P(None, "pairs", None))
    return jax.shard_map(
        body, mesh=mesh, in_specs=placed, out_specs=P("rows", "pairs"), check_vma=False
    )
```

profile of v0, /device:TPU:64, one launch (start us, length us, event | category | flops | bytes accessed | tf_op | source)
XLA Modules:
  0.0 258.2 jit_solution(3819616183086932391)
XLA Ops:
  2.8 3.0 %collective-permute-start.2 = (f32[264,128]{1,0:T(8,128)}, f32[264,128]{1,0:T(8,128)S(1)}, u32[]{:S(2)}, u32[]{:S(2)}) collective-permute-start(f32[264,128]{1,0:T(8,128)} %get-tuple-element.40), channel_id=1, source_target_pairs={{0,192},{16,208},{32,224},{48,240},{64,128},{80,144},{96,160},{112... | collective-permute-start | bytes 405512 | tf_op jit(solution)/shard_map/ppermute | solution.py:213
  6.9 5.0 %collective-permute-done.2 = f32[264,128]{1,0:T(8,128)S(1)} collective-permute-done((f32[264,128]{1,0:T(8,128)}, f32[264,128]{1,0:T(8,128)S(1)}, u32[]{:S(2)}, u32[]{:S(2)}) %collective-permute-start.2) | collective-permute-done | bytes 135200 | tf_op jit(solution)/shard_map/ppermute | solution.py:213
  15.2 4.2 %collective-permute-start.4 = (f32[264,128]{1,0:T(8,128)S(1)}, f32[264,128]{1,0:T(8,128)S(1)}, u32[]{:S(2)}, u32[]{:S(2)}) collective-permute-start(f32[264,128]{1,0:T(8,128)S(1)} %add_add_fusion.9), channel_id=1, source_target_pairs={{0,32},{16,48},{32,0},{48,16},{64,96},{80,112},{96,64},{112,80},{1... | collective-permute-start | bytes 405512 | tf_op jit(solution)/shard_map/ppermute | solution.py:213
  19.4 6.3 %collective-permute-done.5 = f32[264,128]{1,0:T(8,128)S(1)} collective-permute-done((f32[264,128]{1,0:T(8,128)S(1)}, f32[264,128]{1,0:T(8,128)S(1)}, u32[]{:S(2)}, u32[]{:S(2)}) %collective-permute-start.5) | collective-permute-done | bytes 135200 | tf_op jit(solution)/shard_map/ppermute | solution.py:213
  26.4 4.8 %shard_map.29 = (f32[4,64,512]{2,1,0:T(8,128)}, f32[4,64,128]{2,1,0:T(8,128)}) custom-call(bf16[8,64,512]{2,1,0:T(8,128)(2,1)} %get-tuple-element.38.high_ref, bf16[8,64,512]{2,1,0:T(8,128)(2,1)} %get-tuple-element.39.low_ref, f32[264,128]{1,0:T(8,128)} %add_add_fusion.8.sums_ref), custom_call_target="tpu_custom_call" | custom-call | tf_op jit(solution)/shard_map/pallas_call | solution.py:193
  33.5 17.9 %collective-permute-done.6.arrived_ref = f32[4,64,512]{2,1,0:T(8,128)S(1)} collective-permute-done((f32[4,64,512]{2,1,0:T(8,128)}, f32[4,64,512]{2,1,0:T(8,128)S(1)}, u32[]{:S(2)}, u32[]{:S(2)}) %collective-permute-start.6) | collective-permute-done | bytes 524320 | tf_op jit(solution)/shard_map/ppermute | solution.py:239
  54.8 3.3 %collective-permute-start.9 = (f32[264,128]{1,0:T(8,128)}, f32[264,128]{1,0:T(8,128)S(1)}, u32[]{:S(2)}, u32[]{:S(2)}) collective-permute-start(f32[264,128]{1,0:T(8,128)} %get-tuple-element.47), channel_id=1, source_target_pairs={{0,192},{16,208},{32,224},{48,240},{64,128},{80,144},{96,160},{112... | collective-permute-start | bytes 405512 | tf_op jit(solution)/shard_map/ppermute | solution.py:213
  59.0 3.5 %collective-permute-done.9 = f32[264,128]{1,0:T(8,128)S(1)} collective-permute-done((f32[264,128]{1,0:T(8,128)}, f32[264,128]{1,0:T(8,128)S(1)}, u32[]{:S(2)}, u32[]{:S(2)}) %collective-permute-start.9) | collective-permute-done | bytes 135200 | tf_op jit(solution)/shard_map/ppermute | solution.py:213
  66.5 4.9 %collective-permute-start.11 = (f32[264,128]{1,0:T(8,128)S(1)}, f32[264,128]{1,0:T(8,128)S(1)}, u32[]{:S(2)}, u32[]{:S(2)}) collective-permute-start(f32[264,128]{1,0:T(8,128)S(1)} %add_add_fusion.7), channel_id=1, source_target_pairs={{0,32},{16,48},{32,0},{48,16},{64,96},{80,112},{96,64},{112,80},{1... | collective-permute-start | bytes 405512 | tf_op jit(solution)/shard_map/ppermute | solution.py:213
  71.8 4.1 %collective-permute-done.11 = f32[264,128]{1,0:T(8,128)S(1)} collective-permute-done((f32[264,128]{1,0:T(8,128)S(1)}, f32[264,128]{1,0:T(8,128)S(1)}, u32[]{:S(2)}, u32[]{:S(2)}) %collective-permute-start.11) | collective-permute-done | bytes 135200 | tf_op jit(solution)/shard_map/ppermute | solution.py:213
  77.3 4.8 %shard_map.32 = (f32[4,64,512]{2,1,0:T(8,128)}, f32[4,64,128]{2,1,0:T(8,128)}) custom-call(bf16[8,64,512]{2,1,0:T(8,128)(2,1)} %get-tuple-element.45.high_ref, bf16[8,64,512]{2,1,0:T(8,128)(2,1)} %get-tuple-element.46.low_ref, f32[264,128]{1,0:T(8,128)} %add_add_fusion.6.sums_ref), custom_call_target="tpu_custom_call" | custom-call | tf_op jit(solution)/shard_map/pallas_call | solution.py:193
  84.4 17.3 %collective-permute-done.13.arrived_ref = f32[4,64,512]{2,1,0:T(8,128)S(1)} collective-permute-done((f32[4,64,512]{2,1,0:T(8,128)}, f32[4,64,512]{2,1,0:T(8,128)S(1)}, u32[]{:S(2)}, u32[]{:S(2)}) %collective-permute-start.13) | collective-permute-done | bytes 524320 | tf_op jit(solution)/shard_map/ppermute | solution.py:239
  118.8 3.6 %collective-permute-done.19 = f32[264,128]{1,0:T(8,128)S(1)} collective-permute-done((f32[264,128]{1,0:T(8,128)S(1)}, f32[264,128]{1,0:T(8,128)S(1)}, u32[]{:S(2)}, u32[]{:S(2)}) %collective-permute-start.19) | collective-permute-done | bytes 135200 | tf_op jit(solution)/shard_map/ppermute | solution.py:213
  125.2 4.8 %shard_map.35 = (f32[4,64,512]{2,1,0:T(8,128)}, f32[4,64,128]{2,1,0:T(8,128)}) custom-call(bf16[8,64,512]{2,1,0:T(8,128)(2,1)} %get-tuple-element.52.high_ref, bf16[8,64,512]{2,1,0:T(8,128)(2,1)} %get-tuple-element.53.low_ref, f32[264,128]{1,0:T(8,128)} %add_add_fusion.4.sums_ref), custom_call_target="tpu_custom_call" | custom-call | tf_op jit(solution)/shard_map/pallas_call | solution.py:193
  132.3 14.5 %collective-permute-done.20.arrived_ref = f32[4,64,512]{2,1,0:T(8,128)S(1)} collective-permute-done((f32[4,64,512]{2,1,0:T(8,128)}, f32[4,64,512]{2,1,0:T(8,128)S(1)}, u32[]{:S(2)}, u32[]{:S(2)}) %collective-permute-start.20) | collective-permute-done | bytes 524320 | tf_op jit(solution)/shard_map/ppermute | solution.py:239
  152.2 9.9 %collective-permute-start.22 = (f32[264,128]{1,0:T(8,128)}, f32[264,128]{1,0:T(8,128)S(1)}, u32[]{:S(2)}, u32[]{:S(2)}) collective-permute-start(f32[264,128]{1,0:T(8,128)} %get-tuple-element.61), channel_id=1, source_target_pairs={{0,128},{16,144},{32,160},{48,176},{64,192},{80,208},{96,224},{112... | collective-permute-start | bytes 405512 | tf_op jit(solution)/shard_map/ppermute | solution.py:213
  163.3 4.7 %collective-permute-done.22 = f32[264,128]{1,0:T(8,128)S(1)} collective-permute-done((f32[264,128]{1,0:T(8,128)}, f32[264,128]{1,0:T(8,128)S(1)}, u32[]{:S(2)}, u32[]{:S(2)}) %collective-permute-start.22) | collective-permute-done | bytes 135200 | tf_op jit(solution)/shard_map/ppermute | solution.py:213
  168.9 4.5 %collective-permute-start.26 = (f32[264,128]{1,0:T(8,128)S(1)}, f32[264,128]{1,0:T(8,128)S(1)}, u32[]{:S(2)}, u32[]{:S(2)}) collective-permute-start(f32[264,128]{1,0:T(8,128)S(1)} %add_add_fusion.3), channel_id=1, source_target_pairs={{0,48},{16,32},{32,16},{48,0},{64,112},{80,96},{96,80},{112,64},{1... | collective-permute-start | bytes 405512 | tf_op jit(solution)/shard_map/ppermute | solution.py:213
  175.1 3.8 %collective-permute-done.26 = f32[264,128]{1,0:T(8,128)S(1)} collective-permute-done((f32[264,128]{1,0:T(8,128)S(1)}, f32[264,128]{1,0:T(8,128)S(1)}, u32[]{:S(2)}, u32[]{:S(2)}) %collective-permute-start.26) | collective-permute-done | bytes 135200 | tf_op jit(solution)/shard_map/ppermute | solution.py:213
  181.7 4.8 %shard_map.38 = (f32[4,64,512]{2,1,0:T(8,128)}, f32[4,64,128]{2,1,0:T(8,128)}) custom-call(bf16[8,64,512]{2,1,0:T(8,128)(2,1)} %get-tuple-element.59.high_ref, bf16[8,64,512]{2,1,0:T(8,128)(2,1)} %get-tuple-element.60.low_ref, f32[264,128]{1,0:T(8,128)} %add_add_fusion.2.sums_ref), custom_call_target="tpu_custom_call" | custom-call | tf_op jit(solution)/shard_map/pallas_call | solution.py:193
  188.8 17.6 %collective-permute-done.27.arrived_ref = f32[4,64,512]{2,1,0:T(8,128)S(1)} collective-permute-done((f32[4,64,512]{2,1,0:T(8,128)}, f32[4,64,512]{2,1,0:T(8,128)S(1)}, u32[]{:S(2)}, u32[]{:S(2)}) %collective-permute-start.27) | collective-permute-done | bytes 524320 | tf_op jit(solution)/shard_map/ppermute | solution.py:239
  223.1 4.4 %collective-permute-done.33 = f32[264,128]{1,0:T(8,128)S(1)} collective-permute-done((f32[264,128]{1,0:T(8,128)S(1)}, f32[264,128]{1,0:T(8,128)S(1)}, u32[]{:S(2)}, u32[]{:S(2)}) %collective-permute-start.33) | collective-permute-done | bytes 135200 | tf_op jit(solution)/shard_map/ppermute | solution.py:213
  229.5 4.8 %shard_map.41 = (f32[4,64,512]{2,1,0:T(8,128)}, f32[4,64,128]{2,1,0:T(8,128)}) custom-call(bf16[8,64,512]{2,1,0:T(8,128)(2,1)} %get-tuple-element.66.high_ref, bf16[8,64,512]{2,1,0:T(8,128)(2,1)} %get-tuple-element.67.low_ref, f32[264,128]{1,0:T(8,128)} %add_add_fusion.sums_ref), custom_call_target="tpu_custom_call" | custom-call | tf_op jit(solution)/shard_map/pallas_call | solution.py:193
  236.6 18.1 %collective-permute-done.34.arrived_ref = f32[4,64,512]{2,1,0:T(8,128)S(1)} collective-permute-done((f32[4,64,512]{2,1,0:T(8,128)}, f32[4,64,512]{2,1,0:T(8,128)S(1)}, u32[]{:S(2)}, u32[]{:S(2)}) %collective-permute-start.34) | collective-permute-done | bytes 524320 | tf_op jit(solution)/shard_map/ppermute | solution.py:239
  (82 shorter events, 83.7 us)
Async XLA Ops:
  2.8 9.1 %collective-permute-start.2 = (f32[264,128]{1,0:T(8,128)}, f32[264,128]{1,0:T(8,128)S(1)}, u32[]{:S(2)}, u32[]{:S(2)}) collective-permute-start(f32[264,128]{1,0:T(8,128)} %get-tuple-element.40), channel_id=1, source_target_pairs={{0,192},{16,208},{32,224},{48,240},{64,128},{80,144},{96,160},{112... | collective-permute-start | bytes 405512 | tf_op jit(solution)/shard_map/ppermute | solution.py:213
  5.9 8.2 %collective-permute-start.1 = (f32[264,128]{1,0:T(8,128)}, f32[264,128]{1,0:T(8,128)S(1)}, u32[]{:S(2)}, u32[]{:S(2)}) collective-permute-start(f32[264,128]{1,0:T(8,128)} %get-tuple-element.40), channel_id=1, source_target_pairs={{0,128},{16,144},{32,160},{48,176},{64,192},{80,208},{96,224},{112... | collective-permute-start | bytes 405512 | tf_op jit(solution)/shard_map/ppermute | solution.py:213
  6.5 7.6 %collective-permute-start = (f32[264,128]{1,0:T(8,128)}, f32[264,128]{1,0:T(8,128)S(1)}, u32[]{:S(2)}, u32[]{:S(2)}) collective-permute-start(f32[264,128]{1,0:T(8,128)} %get-tuple-element.40), channel_id=1, source_target_pairs={{0,64},{16,80},{32,96},{48,112},{64,0},{80,16},{96,32},{112,48},{1... | collective-permute-start | bytes 405512 | tf_op jit(solution)/shard_map/ppermute | solution.py:213
  15.0 10.7 %collective-permute-start.5 = (f32[264,128]{1,0:T(8,128)S(1)}, f32[264,128]{1,0:T(8,128)S(1)}, u32[]{:S(2)}, u32[]{:S(2)}) collective-permute-start(f32[264,128]{1,0:T(8,128)S(1)} %add_add_fusion.9), channel_id=1, source_target_pairs={{0,48},{16,32},{32,16},{48,0},{64,112},{80,96},{96,80},{112,64},{1... | collective-permute-start | bytes 405512 | tf_op jit(solution)/shard_map/ppermute | solution.py:213
  15.2 10.5 %collective-permute-start.4 = (f32[264,128]{1,0:T(8,128)S(1)}, f32[264,128]{1,0:T(8,128)S(1)}, u32[]{:S(2)}, u32[]{:S(2)}) collective-permute-start(f32[264,128]{1,0:T(8,128)S(1)} %add_add_fusion.9), channel_id=1, source_target_pairs={{0,32},{16,48},{32,0},{48,16},{64,96},{80,112},{96,64},{112,80},{1... | collective-permute-start | bytes 405512 | tf_op jit(solution)/shard_map/ppermute | solution.py:213
  31.2 20.3 %collective-permute-start.6 = (f32[4,64,512]{2,1,0:T(8,128)}, f32[4,64,512]{2,1,0:T(8,128)S(1)}, u32[]{:S(2)}, u32[]{:S(2)}) collective-permute-start(f32[4,64,512]{2,1,0:T(8,128)} %get-tuple-element.44), channel_id=1, source_target_pairs={{0,1},{1,2},{2,3},{3,4},{4,5},{5,6},{6,7},{7,8},{8,9},{9,10},{10,1... | collective-permute-start | bytes 1572872 | tf_op jit(solution)/shard_map/ppermute | solution.py:239
  54.8 7.6 %collective-permute-start.9 = (f32[264,128]{1,0:T(8,128)}, f32[264,128]{1,0:T(8,128)S(1)}, u32[]{:S(2)}, u32[]{:S(2)}) collective-permute-start(f32[264,128]{1,0:T(8,128)} %get-tuple-element.47), channel_id=1, source_target_pairs={{0,192},{16,208},{32,224},{48,240},{64,128},{80,144},{96,160},{112... | collective-permute-start | bytes 405512 | tf_op jit(solution)/shard_map/ppermute | solution.py:213
  58.1 6.7 %collective-permute-start.8 = (f32[264,128]{1,0:T(8,128)}, f32[264,128]{1,0:T(8,128)S(1)}, u32[]{:S(2)}, u32[]{:S(2)}) collective-permute-start(f32[264,128]{1,0:T(8,128)} %get-tuple-element.47), channel_id=1, source_target_pairs={{0,128},{16,144},{32,160},{48,176},{64,192},{80,208},{96,224},{112... | collective-permute-start | bytes 405512 | tf_op jit(solution)/shard_map/ppermute | solution.py:213
  66.5 9.4 %collective-permute-start.11 = (f32[264,128]{1,0:T(8,128)S(1)}, f32[264,128]{1,0:T(8,128)S(1)}, u32[]{:S(2)}, u32[]{:S(2)}) collective-permute-start(f32[264,128]{1,0:T(8,128)S(1)} %add_add_fusion.7), channel_id=1, source_target_pairs={{0,32},{16,48},{32,0},{48,16},{64,96},{80,112},{96,64},{112,80},{1... | collective-permute-start | bytes 405512 | tf_op jit(solution)/shard_map/ppermute | solution.py:213
  82.1 19.6 %collective-permute-start.13 = (f32[4,64,512]{2,1,0:T(8,128)}, f32[4,64,512]{2,1,0:T(8,128)S(1)}, u32[]{:S(2)}, u32[]{:S(2)}) collective-permute-start(f32[4,64,512]{2,1,0:T(8,128)} %get-tuple-element.51), channel_id=1, source_target_pairs={{0,1},{1,2},{2,3},{3,4},{4,5},{5,6},{6,7},{7,8},{8,9},{9,10},{10,1... | collective-permute-start | bytes 1572872 | tf_op jit(solution)/shard_map/ppermute | solution.py:239
  107.1 6.7 %collective-permute-start.15 = (f32[264,128]{1,0:T(8,128)}, f32[264,128]{1,0:T(8,128)S(1)}, u32[]{:S(2)}, u32[]{:S(2)}) collective-permute-start(f32[264,128]{1,0:T(8,128)} %get-tuple-element.54), channel_id=1, source_target_pairs={{0,128},{16,144},{32,160},{48,176},{64,192},{80,208},{96,224},{112... | collective-permute-start | bytes 405512 | tf_op jit(solution)/shard_map/ppermute | solution.py:213
  114.8 7.6 %collective-permute-start.19 = (f32[264,128]{1,0:T(8,128)S(1)}, f32[264,128]{1,0:T(8,128)S(1)}, u32[]{:S(2)}, u32[]{:S(2)}) collective-permute-start(f32[264,128]{1,0:T(8,128)S(1)} %add_add_fusion.5), channel_id=1, source_target_pairs={{0,48},{16,32},{32,16},{48,0},{64,112},{80,96},{96,80},{112,64},{1... | collective-permute-start | bytes 405512 | tf_op jit(solution)/shard_map/ppermute | solution.py:213
  116.9 6.9 %collective-permute-start.18 = (f32[264,128]{1,0:T(8,128)S(1)}, f32[264,128]{1,0:T(8,128)S(1)}, u32[]{:S(2)}, u32[]{:S(2)}) collective-permute-start(f32[264,128]{1,0:T(8,128)S(1)} %add_add_fusion.5), channel_id=1, source_target_pairs={{0,32},{16,48},{32,0},{48,16},{64,96},{80,112},{96,64},{112,80},{1... | collective-permute-start | bytes 405512 | tf_op jit(solution)/shard_map/ppermute | solution.py:213
  130.0 16.8 %collective-permute-start.20 = (f32[4,64,512]{2,1,0:T(8,128)}, f32[4,64,512]{2,1,0:T(8,128)S(1)}, u32[]{:S(2)}, u32[]{:S(2)}) collective-permute-start(f32[4,64,512]{2,1,0:T(8,128)} %get-tuple-element.58), channel_id=1, source_target_pairs={{0,1},{1,2},{2,3},{3,4},{4,5},{5,6},{6,7},{7,8},{8,9},{9,10},{10,1... | collective-permute-start | bytes 1572872 | tf_op jit(solution)/shard_map/ppermute | solution.py:239
  150.2 13.1 %collective-permute-start.23 = (f32[264,128]{1,0:T(8,128)}, f32[264,128]{1,0:T(8,128)S(1)}, u32[]{:S(2)}, u32[]{:S(2)}) collective-permute-start(f32[264,128]{1,0:T(8,128)} %get-tuple-element.61), channel_id=1, source_target_pairs={{0,192},{16,208},{32,224},{48,240},{64,128},{80,144},{96,160},{112... | collective-permute-start | bytes 405512 | tf_op jit(solution)/shard_map/ppermute | solution.py:213
  152.2 15.7 %collective-permute-start.22 = (f32[264,128]{1,0:T(8,128)}, f32[264,128]{1,0:T(8,128)S(1)}, u32[]{:S(2)}, u32[]{:S(2)}) collective-permute-start(f32[264,128]{1,0:T(8,128)} %get-tuple-element.61), channel_id=1, source_target_pairs={{0,128},{16,144},{32,160},{48,176},{64,192},{80,208},{96,224},{112... | collective-permute-start | bytes 405512 | tf_op jit(solution)/shard_map/ppermute | solution.py:213
  168.9 9.9 %collective-permute-start.26 = (f32[264,128]{1,0:T(8,128)S(1)}, f32[264,128]{1,0:T(8,128)S(1)}, u32[]{:S(2)}, u32[]{:S(2)}) collective-permute-start(f32[264,128]{1,0:T(8,128)S(1)} %add_add_fusion.3), channel_id=1, source_target_pairs={{0,48},{16,32},{32,16},{48,0},{64,112},{80,96},{96,80},{112,64},{1... | collective-permute-start | bytes 405512 | tf_op jit(solution)/shard_map/ppermute | solution.py:213
  173.4 6.9 %collective-permute-start.25 = (f32[264,128]{1,0:T(8,128)S(1)}, f32[264,128]{1,0:T(8,128)S(1)}, u32[]{:S(2)}, u32[]{:S(2)}) collective-permute-start(f32[264,128]{1,0:T(8,128)S(1)} %add_add_fusion.3), channel_id=1, source_target_pairs={{0,32},{16,48},{32,0},{48,16},{64,96},{80,112},{96,64},{112,80},{1... | collective-permute-start | bytes 405512 | tf_op jit(solution)/shard_map/ppermute | solution.py:213
  186.4 20.0 %collective-permute-start.27 = (f32[4,64,512]{2,1,0:T(8,128)}, f32[4,64,512]{2,1,0:T(8,128)S(1)}, u32[]{:S(2)}, u32[]{:S(2)}) collective-permute-start(f32[4,64,512]{2,1,0:T(8,128)} %get-tuple-element.65), channel_id=1, source_target_pairs={{0,1},{1,2},{2,3},{3,4},{4,5},{5,6},{6,7},{7,8},{8,9},{9,10},{10,1... | collective-permute-start | bytes 1572872 | tf_op jit(solution)/shard_map/ppermute | solution.py:239
  211.7 6.7 %collective-permute-start.29 = (f32[264,128]{1,0:T(8,128)}, f32[264,128]{1,0:T(8,128)S(1)}, u32[]{:S(2)}, u32[]{:S(2)}) collective-permute-start(f32[264,128]{1,0:T(8,128)} %get-tuple-element.68), channel_id=1, source_target_pairs={{0,128},{16,144},{32,160},{48,176},{64,192},{80,208},{96,224},{112... | collective-permute-start | bytes 405512 | tf_op jit(solution)/shard_map/ppermute | solution.py:213
  212.0 6.5 %collective-permute-start.28 = (f32[264,128]{1,0:T(8,128)}, f32[264,128]{1,0:T(8,128)S(1)}, u32[]{:S(2)}, u32[]{:S(2)}) collective-permute-start(f32[264,128]{1,0:T(8,128)} %get-tuple-element.68), channel_id=1, source_target_pairs={{0,64},{16,80},{32,96},{48,112},{64,0},{80,16},{96,32},{112,48},{1... | collective-permute-start | bytes 405512 | tf_op jit(solution)/shard_map/ppermute | solution.py:213
  219.5 8.0 %collective-permute-start.33 = (f32[264,128]{1,0:T(8,128)S(1)}, f32[264,128]{1,0:T(8,128)S(1)}, u32[]{:S(2)}, u32[]{:S(2)}) collective-permute-start(f32[264,128]{1,0:T(8,128)S(1)} %add_add_fusion.1), channel_id=1, source_target_pairs={{0,48},{16,32},{32,16},{48,0},{64,112},{80,96},{96,80},{112,64},{1... | collective-permute-start | bytes 405512 | tf_op jit(solution)/shard_map/ppermute | solution.py:213
  220.6 7.2 %collective-permute-start.32 = (f32[264,128]{1,0:T(8,128)S(1)}, f32[264,128]{1,0:T(8,128)S(1)}, u32[]{:S(2)}, u32[]{:S(2)}) collective-permute-start(f32[264,128]{1,0:T(8,128)S(1)} %add_add_fusion.1), channel_id=1, source_target_pairs={{0,32},{16,48},{32,0},{48,16},{64,96},{80,112},{96,64},{112,80},{1... | collective-permute-start | bytes 405512 | tf_op jit(solution)/shard_map/ppermute | solution.py:213
  234.2 20.5 %collective-permute-start.34 = (f32[4,64,512]{2,1,0:T(8,128)}, f32[4,64,512]{2,1,0:T(8,128)S(1)}, u32[]{:S(2)}, u32[]{:S(2)}) collective-permute-start(f32[4,64,512]{2,1,0:T(8,128)} %get-tuple-element.70), channel_id=1, source_target_pairs={{0,1},{1,2},{2,3},{3,4},{4,5},{5,6},{6,7},{7,8},{8,9},{9,10},{10,1... | collective-permute-start | bytes 1572872 | tf_op jit(solution)/shard_map/ppermute | solution.py:239
  (16 other events, 70.9 us)
where the time goes:
time: 262 us; the launch traced here: 258 us
  waiting for transfers between devices  141 us (54%)
  starting transfers between devices  53.5 us (20%)
  Pallas kernels  51.2 us (20%)
  other arithmetic  8.12 us (3%)
  local copies, waits for them, and re-layouts  3.96 us (2%)
    ppermute x5, waiting for transfers between devices, body(): arrived = lax.ppermute(move, 'pairs', along)  85.5 us
    ppermute x30, waiting for transfers between devices, from_four(): lax.ppermute(value, 'rows', [(r, other(r, d)) for r in rows])  55.6 us
    ppermute x30, starting transfers between devices, from_four(): lax.ppermute(value, 'rows', [(r, other(r, d)) for r in rows])  53.5 us
    pallas_call x16, Pallas kernels, call(): pl.pallas_call(kernel, out_shape=shapes, in_specs=[SMEM if x.dtype == jnp...  51.2 us
    add x10, other arithmetic, four(): return a + b + (c + d)  8.12 us
  transfers between devices with their start and end apart: 35, of which 28 were waited for; matrix products, arithmetic and copies ran while one was open for 0% of the time, Pallas kernels for 5%

commit v1 on v0

--- a/solution.py
+++ b/solution.py
@@ -11,6 +11,7 @@
 WIDE = 2 * BLK
 ROUNDS = 5
 NS_STEPS = 6
+ROOM = 16 << 20
 
 VMEM = pl.BlockSpec(memory_space=pltpu.VMEM)
 SMEM = pl.BlockSpec(memory_space=pltpu.SMEM)
@@ -196,6 +197,7 @@
         in_specs=[SMEM if x.dtype == jnp.int32 else VMEM for x in operands],
         out_specs=jax.tree.map(lambda _: VMEM, shapes),
         scratch_shapes=scratch,
+        compiler_params=pltpu.CompilerParams(vmem_limit_bytes=ROOM),
     )(*operands)
 
 

time: 262 us -> 221 us (0.84); the launches traced: 258 us -> 220 us
  Pallas kernels: 51.2 us -> 23.4 us
  other arithmetic: 8.12 us -> 0.31 us
  starting transfers between devices: 53.5 us -> 47.5 us
  waiting for transfers between devices: 141 us -> 147 us
    pallas_call x16, Pallas kernels: 51.2 us -> 23.4 us  [call(): pl.pallas_call(kernel, out_shape=shapes, in_specs=[SMEM if x.dtype == jnp...]
    add x10, other arithmetic: 8.12 us -> 0.31 us  [four(): return a + b + (c + d)]
    ppermute x5, waiting for transfers between devices: 85.5 us -> 92 us  [body(): arrived = lax.ppermute(move, 'pairs', along)]
    ppermute x30, starting transfers between devices: 53.5 us -> 47.1 us  [from_four(): lax.ppermute(value, 'rows', [(r, other(r, d)) for r in rows])]
  transfers between devices with their start and end apart: 35 -> 35, of which waited for: 28 -> 28; matrix products, arithmetic and copies ran while one was open for 0% -> 0% of each run, Pallas kernels for 5% -> 1%
where the time goes in v1:
time: 221 us; the launch traced here: 220 us
  waiting for transfers between devices  147 us (67%)
  starting transfers between devices  47.5 us (21%)
  Pallas kernels  23.4 us (11%)
    ppermute x5, waiting for transfers between devices, body(): arrived = lax.ppermute(move, 'pairs', along)  92 us
    ppermute x30, waiting for transfers between devices, from_four(): lax.ppermute(value, 'rows', [(r, other(r, d)) for r in rows])  54.9 us
    ppermute x30, starting transfers between devices, from_four(): lax.ppermute(value, 'rows', [(r, other(r, d)) for r in rows])  47.1 us
    pallas_call x16, Pallas kernels, call(): pl.pallas_call(kernel, out_shape=shapes, in_specs=[SMEM if x.dtype == jnp...  23.4 us
  transfers between devices with their start and end apart: 35, of which 28 were waited for; matrix products, arithmetic and copies ran while one was open for 0% of the time, Pallas kernels for 1%

profile of v1, /device:TPU:64, one launch (start us, length us, event | category | flops | bytes accessed | tf_op | source)
XLA Modules:
  0.0 220.1 jit_solution(3133373482346006745)
XLA Ops:
  3.4 3.1 %collective-permute-start.2 = (f32[264,128]{1,0:T(8,128)S(1)}, f32[264,128]{1,0:T(8,128)S(1)}, u32[]{:S(2)}, u32[]{:S(2)}) collective-permute-start(f32[264,128]{1,0:T(8,128)S(1)} %get-tuple-element.40), channel_id=1, source_target_pairs={{0,192},{16,208},{32,224},{48,240},{64,128},{80,144},{96,160},{112... | collective-permute-start | bytes 405512 | tf_op jit(solution)/shard_map/ppermute | solution.py:215
  7.6 4.7 %collective-permute-done.2 = f32[264,128]{1,0:T(8,128)S(1)} collective-permute-done((f32[264,128]{1,0:T(8,128)S(1)}, f32[264,128]{1,0:T(8,128)S(1)}, u32[]{:S(2)}, u32[]{:S(2)}) %collective-permute-start.2) | collective-permute-done | bytes 135200 | tf_op jit(solution)/shard_map/ppermute | solution.py:215
  14.8 4.2 %collective-permute-start.4 = (f32[264,128]{1,0:T(8,128)S(1)}, f32[264,128]{1,0:T(8,128)S(1)}, u32[]{:S(2)}, u32[]{:S(2)}) collective-permute-start(f32[264,128]{1,0:T(8,128)S(1)} %add_add_fusion.9), channel_id=1, source_target_pairs={{0,32},{16,48},{32,0},{48,16},{64,96},{80,112},{96,64},{112,80},{1... | collective-permute-start | bytes 405512 | tf_op jit(solution)/shard_map/ppermute | solution.py:215
  18.9 6.5 %collective-permute-done.5 = f32[264,128]{1,0:T(8,128)S(1)} collective-permute-done((f32[264,128]{1,0:T(8,128)S(1)}, f32[264,128]{1,0:T(8,128)S(1)}, u32[]{:S(2)}, u32[]{:S(2)}) %collective-permute-start.5) | collective-permute-done | bytes 135200 | tf_op jit(solution)/shard_map/ppermute | solution.py:215
  25.5 2.7 %shard_map.29 = (f32[4,64,512]{2,1,0:T(8,128)S(1)}, f32[4,64,128]{2,1,0:T(8,128)S(1)}) custom-call(bf16[8,64,512]{2,1,0:T(8,128)(2,1)S(1)} %get-tuple-element.38.high_ref, bf16[8,64,512]{2,1,0:T(8,128)(2,1)S(1)} %get-tuple-element.39.low_ref, f32[264,128]{1,0:T(8,128)S(1)} %add_add_fusion.8.sums_ref), custom_call_target="tpu_custom_call" | custom-call | tf_op jit(solution)/shard_map/pallas_call | solution.py:194
  28.7 19.8 %collective-permute-done.6.arrived_ref = f32[4,64,512]{2,1,0:T(8,128)S(1)} collective-permute-done((f32[4,64,512]{2,1,0:T(8,128)S(1)}, f32[4,64,512]{2,1,0:T(8,128)S(1)}, u32[]{:S(2)}, u32[]{:S(2)}) %collective-permute-start.6) | collective-permute-done | bytes 524320 | tf_op jit(solution)/shard_map/ppermute | solution.py:241
  49.7 3.0 %collective-permute-start.9 = (f32[264,128]{1,0:T(8,128)S(1)}, f32[264,128]{1,0:T(8,128)S(1)}, u32[]{:S(2)}, u32[]{:S(2)}) collective-permute-start(f32[264,128]{1,0:T(8,128)S(1)} %get-tuple-element.47), channel_id=1, source_target_pairs={{0,192},{16,208},{32,224},{48,240},{64,128},{80,144},{96,160},{112... | collective-permute-start | bytes 405512 | tf_op jit(solution)/shard_map/ppermute | solution.py:215
  53.9 2.9 %collective-permute-done.9 = f32[264,128]{1,0:T(8,128)S(1)} collective-permute-done((f32[264,128]{1,0:T(8,128)S(1)}, f32[264,128]{1,0:T(8,128)S(1)}, u32[]{:S(2)}, u32[]{:S(2)}) %collective-permute-start.9) | collective-permute-done | bytes 135200 | tf_op jit(solution)/shard_map/ppermute | solution.py:215
  56.8 2.5 %collective-permute-done.8 = f32[264,128]{1,0:T(8,128)S(1)} collective-permute-done((f32[264,128]{1,0:T(8,128)S(1)}, f32[264,128]{1,0:T(8,128)S(1)}, u32[]{:S(2)}, u32[]{:S(2)}) %collective-permute-start.8) | collective-permute-done | bytes 135200 | tf_op jit(solution)/shard_map/ppermute | solution.py:215
  60.1 4.9 %collective-permute-start.11 = (f32[264,128]{1,0:T(8,128)S(1)}, f32[264,128]{1,0:T(8,128)S(1)}, u32[]{:S(2)}, u32[]{:S(2)}) collective-permute-start(f32[264,128]{1,0:T(8,128)S(1)} %add_add_fusion.7), channel_id=1, source_target_pairs={{0,32},{16,48},{32,0},{48,16},{64,96},{80,112},{96,64},{112,80},{1... | collective-permute-start | bytes 405512 | tf_op jit(solution)/shard_map/ppermute | solution.py:215
  65.3 4.2 %collective-permute-done.11 = f32[264,128]{1,0:T(8,128)S(1)} collective-permute-done((f32[264,128]{1,0:T(8,128)S(1)}, f32[264,128]{1,0:T(8,128)S(1)}, u32[]{:S(2)}, u32[]{:S(2)}) %collective-permute-start.11) | collective-permute-done | bytes 135200 | tf_op jit(solution)/shard_map/ppermute | solution.py:215
  70.0 2.7 %shard_map.32 = (f32[4,64,512]{2,1,0:T(8,128)S(1)}, f32[4,64,128]{2,1,0:T(8,128)S(1)}) custom-call(bf16[8,64,512]{2,1,0:T(8,128)(2,1)S(1)} %get-tuple-element.45.high_ref, bf16[8,64,512]{2,1,0:T(8,128)(2,1)S(1)} %get-tuple-element.46.low_ref, f32[264,128]{1,0:T(8,128)S(1)} %add_add_fusion.6.sums_ref), custom_call_target="tpu_custom_call" | custom-call | tf_op jit(solution)/shard_map/pallas_call | solution.py:194
  73.2 16.6 %collective-permute-done.13.arrived_ref = f32[4,64,512]{2,1,0:T(8,128)S(1)} collective-permute-done((f32[4,64,512]{2,1,0:T(8,128)S(1)}, f32[4,64,512]{2,1,0:T(8,128)S(1)}, u32[]{:S(2)}, u32[]{:S(2)}) %collective-permute-start.13) | collective-permute-done | bytes 524320 | tf_op jit(solution)/shard_map/ppermute | solution.py:241
  99.8 4.8 %collective-permute-start.19 = (f32[264,128]{1,0:T(8,128)S(1)}, f32[264,128]{1,0:T(8,128)S(1)}, u32[]{:S(2)}, u32[]{:S(2)}) collective-permute-start(f32[264,128]{1,0:T(8,128)S(1)} %add_add_fusion.5), channel_id=1, source_target_pairs={{0,48},{16,32},{32,16},{48,0},{64,112},{80,96},{96,80},{112,64},{1... | collective-permute-start | bytes 405512 | tf_op jit(solution)/shard_map/ppermute | solution.py:215
  106.3 3.8 %collective-permute-done.19 = f32[264,128]{1,0:T(8,128)S(1)} collective-permute-done((f32[264,128]{1,0:T(8,128)S(1)}, f32[264,128]{1,0:T(8,128)S(1)}, u32[]{:S(2)}, u32[]{:S(2)}) %collective-permute-start.19) | collective-permute-done | bytes 135200 | tf_op jit(solution)/shard_map/ppermute | solution.py:215
  112.2 2.7 %shard_map.35 = (f32[4,64,512]{2,1,0:T(8,128)S(1)}, f32[4,64,128]{2,1,0:T(8,128)S(1)}) custom-call(bf16[8,64,512]{2,1,0:T(8,128)(2,1)S(1)} %get-tuple-element.52.high_ref, bf16[8,64,512]{2,1,0:T(8,128)(2,1)S(1)} %get-tuple-element.53.low_ref, f32[264,128]{1,0:T(8,128)S(1)} %add_add_fusion.4.sums_ref), custom_call_target="tpu_custom_call" | custom-call | tf_op jit(solution)/shard_map/pallas_call | solution.py:194
  115.4 16.3 %collective-permute-done.20.arrived_ref = f32[4,64,512]{2,1,0:T(8,128)S(1)} collective-permute-done((f32[4,64,512]{2,1,0:T(8,128)S(1)}, f32[4,64,512]{2,1,0:T(8,128)S(1)}, u32[]{:S(2)}, u32[]{:S(2)}) %collective-permute-start.20) | collective-permute-done | bytes 524320 | tf_op jit(solution)/shard_map/ppermute | solution.py:241
  142.6 5.0 %collective-permute-start.25 = (f32[264,128]{1,0:T(8,128)S(1)}, f32[264,128]{1,0:T(8,128)S(1)}, u32[]{:S(2)}, u32[]{:S(2)}) collective-permute-start(f32[264,128]{1,0:T(8,128)S(1)} %add_add_fusion.3), channel_id=1, source_target_pairs={{0,32},{16,48},{32,0},{48,16},{64,96},{80,112},{96,64},{112,80},{1... | collective-permute-start | bytes 405512 | tf_op jit(solution)/shard_map/ppermute | solution.py:215
  147.8 4.9 %collective-permute-done.25 = f32[264,128]{1,0:T(8,128)S(1)} collective-permute-done((f32[264,128]{1,0:T(8,128)S(1)}, f32[264,128]{1,0:T(8,128)S(1)}, u32[]{:S(2)}, u32[]{:S(2)}) %collective-permute-start.25) | collective-permute-done | bytes 135200 | tf_op jit(solution)/shard_map/ppermute | solution.py:215
  153.8 2.7 %shard_map.38 = (f32[4,64,512]{2,1,0:T(8,128)S(1)}, f32[4,64,128]{2,1,0:T(8,128)S(1)}) custom-call(bf16[8,64,512]{2,1,0:T(8,128)(2,1)S(1)} %get-tuple-element.59.high_ref, bf16[8,64,512]{2,1,0:T(8,128)(2,1)S(1)} %get-tuple-element.60.low_ref, f32[264,128]{1,0:T(8,128)S(1)} %add_add_fusion.2.sums_ref), custom_call_target="tpu_custom_call" | custom-call | tf_op jit(solution)/shard_map/pallas_call | solution.py:194
  156.9 19.4 %collective-permute-done.27.arrived_ref = f32[4,64,512]{2,1,0:T(8,128)S(1)} collective-permute-done((f32[4,64,512]{2,1,0:T(8,128)S(1)}, f32[4,64,512]{2,1,0:T(8,128)S(1)}, u32[]{:S(2)}, u32[]{:S(2)}) %collective-permute-start.27) | collective-permute-done | bytes 524320 | tf_op jit(solution)/shard_map/ppermute | solution.py:241
  189.8 4.4 %collective-permute-done.33 = f32[264,128]{1,0:T(8,128)S(1)} collective-permute-done((f32[264,128]{1,0:T(8,128)S(1)}, f32[264,128]{1,0:T(8,128)S(1)}, u32[]{:S(2)}, u32[]{:S(2)}) %collective-permute-start.33) | collective-permute-done | bytes 135200 | tf_op jit(solution)/shard_map/ppermute | solution.py:215
  195.7 2.7 %shard_map.41 = (f32[4,64,512]{2,1,0:T(8,128)S(1)}, f32[4,64,128]{2,1,0:T(8,128)S(1)}) custom-call(bf16[8,64,512]{2,1,0:T(8,128)(2,1)S(1)} %get-tuple-element.66.high_ref, bf16[8,64,512]{2,1,0:T(8,128)(2,1)S(1)} %get-tuple-element.67.low_ref, f32[264,128]{1,0:T(8,128)S(1)} %add_add_fusion.sums_ref), custom_call_target="tpu_custom_call" | custom-call | tf_op jit(solution)/shard_map/pallas_call | solution.py:194
  198.8 20.0 %collective-permute-done.34.arrived_ref = f32[4,64,512]{2,1,0:T(8,128)S(1)} collective-permute-done((f32[4,64,512]{2,1,0:T(8,128)S(1)}, f32[4,64,512]{2,1,0:T(8,128)S(1)}, u32[]{:S(2)}, u32[]{:S(2)}) %collective-permute-start.34) | collective-permute-done | bytes 524320 | tf_op jit(solution)/shard_map/ppermute | solution.py:241
  (76 shorter events, 55.4 us)
Async XLA Ops:
  3.4 8.9 %collective-permute-start.2 = (f32[264,128]{1,0:T(8,128)S(1)}, f32[264,128]{1,0:T(8,128)S(1)}, u32[]{:S(2)}, u32[]{:S(2)}) collective-permute-start(f32[264,128]{1,0:T(8,128)S(1)} %get-tuple-element.40), channel_id=1, source_target_pairs={{0,192},{16,208},{32,224},{48,240},{64,128},{80,144},{96,160},{112... | collective-permute-start | bytes 405512 | tf_op jit(solution)/shard_map/ppermute | solution.py:215
  6.5 8.0 %collective-permute-start.1 = (f32[264,128]{1,0:T(8,128)S(1)}, f32[264,128]{1,0:T(8,128)S(1)}, u32[]{:S(2)}, u32[]{:S(2)}) collective-permute-start(f32[264,128]{1,0:T(8,128)S(1)} %get-tuple-element.40), channel_id=1, source_target_pairs={{0,128},{16,144},{32,160},{48,176},{64,192},{80,208},{96,224},{112... | collective-permute-start | bytes 405512 | tf_op jit(solution)/shard_map/ppermute | solution.py:215
  7.2 7.4 %collective-permute-start = (f32[264,128]{1,0:T(8,128)S(1)}, f32[264,128]{1,0:T(8,128)S(1)}, u32[]{:S(2)}, u32[]{:S(2)}) collective-permute-start(f32[264,128]{1,0:T(8,128)S(1)} %get-tuple-element.40), channel_id=1, source_target_pairs={{0,64},{16,80},{32,96},{48,112},{64,0},{80,16},{96,32},{112,48},{1... | collective-permute-start | bytes 405512 | tf_op jit(solution)/shard_map/ppermute | solution.py:215
  14.6 10.9 %collective-permute-start.5 = (f32[264,128]{1,0:T(8,128)S(1)}, f32[264,128]{1,0:T(8,128)S(1)}, u32[]{:S(2)}, u32[]{:S(2)}) collective-permute-start(f32[264,128]{1,0:T(8,128)S(1)} %add_add_fusion.9), channel_id=1, source_target_pairs={{0,48},{16,32},{32,16},{48,0},{64,112},{80,96},{96,80},{112,64},{1... | collective-permute-start | bytes 405512 | tf_op jit(solution)/shard_map/ppermute | solution.py:215
  14.8 10.7 %collective-permute-start.4 = (f32[264,128]{1,0:T(8,128)S(1)}, f32[264,128]{1,0:T(8,128)S(1)}, u32[]{:S(2)}, u32[]{:S(2)}) collective-permute-start(f32[264,128]{1,0:T(8,128)S(1)} %add_add_fusion.9), channel_id=1, source_target_pairs={{0,32},{16,48},{32,0},{48,16},{64,96},{80,112},{96,64},{112,80},{1... | collective-permute-start | bytes 405512 | tf_op jit(solution)/shard_map/ppermute | solution.py:215
  18.9 6.5 %collective-permute-start.3 = (f32[264,128]{1,0:T(8,128)S(1)}, f32[264,128]{1,0:T(8,128)S(1)}, u32[]{:S(2)}, u32[]{:S(2)}) collective-permute-start(f32[264,128]{1,0:T(8,128)S(1)} %add_add_fusion.9), channel_id=1, source_target_pairs={{0,16},{16,0},{32,48},{48,32},{64,80},{80,64},{96,112},{112,96},{1... | collective-permute-start | bytes 405512 | tf_op jit(solution)/shard_map/ppermute | solution.py:215
  28.3 20.2 %collective-permute-start.6 = (f32[4,64,512]{2,1,0:T(8,128)S(1)}, f32[4,64,512]{2,1,0:T(8,128)S(1)}, u32[]{:S(2)}, u32[]{:S(2)}) collective-permute-start(f32[4,64,512]{2,1,0:T(8,128)S(1)} %get-tuple-element.44), channel_id=1, source_target_pairs={{0,1},{1,2},{2,3},{3,4},{4,5},{5,6},{6,7},{7,8},{8,9},{9,10},{10,1... | collective-permute-start | bytes 1572872 | tf_op jit(solution)/shard_map/ppermute | solution.py:241
  49.7 7.1 %collective-permute-start.9 = (f32[264,128]{1,0:T(8,128)S(1)}, f32[264,128]{1,0:T(8,128)S(1)}, u32[]{:S(2)}, u32[]{:S(2)}) collective-permute-start(f32[264,128]{1,0:T(8,128)S(1)} %get-tuple-element.47), channel_id=1, source_target_pairs={{0,192},{16,208},{32,224},{48,240},{64,128},{80,144},{96,160},{112... | collective-permute-start | bytes 405512 | tf_op jit(solution)/shard_map/ppermute | solution.py:215
  52.8 6.5 %collective-permute-start.8 = (f32[264,128]{1,0:T(8,128)S(1)}, f32[264,128]{1,0:T(8,128)S(1)}, u32[]{:S(2)}, u32[]{:S(2)}) collective-permute-start(f32[264,128]{1,0:T(8,128)S(1)} %get-tuple-element.47), channel_id=1, source_target_pairs={{0,128},{16,144},{32,160},{48,176},{64,192},{80,208},{96,224},{112... | collective-permute-start | bytes 405512 | tf_op jit(solution)/shard_map/ppermute | solution.py:215
  60.1 9.4 %collective-permute-start.11 = (f32[264,128]{1,0:T(8,128)S(1)}, f32[264,128]{1,0:T(8,128)S(1)}, u32[]{:S(2)}, u32[]{:S(2)}) collective-permute-start(f32[264,128]{1,0:T(8,128)S(1)} %add_add_fusion.7), channel_id=1, source_target_pairs={{0,32},{16,48},{32,0},{48,16},{64,96},{80,112},{96,64},{112,80},{1... | collective-permute-start | bytes 405512 | tf_op jit(solution)/shard_map/ppermute | solution.py:215
  72.7 17.0 %collective-permute-start.13 = (f32[4,64,512]{2,1,0:T(8,128)S(1)}, f32[4,64,512]{2,1,0:T(8,128)S(1)}, u32[]{:S(2)}, u32[]{:S(2)}) collective-permute-start(f32[4,64,512]{2,1,0:T(8,128)S(1)} %get-tuple-element.51), channel_id=1, source_target_pairs={{0,1},{1,2},{2,3},{3,4},{4,5},{5,6},{6,7},{7,8},{8,9},{9,10},{10,1... | collective-permute-start | bytes 1572872 | tf_op jit(solution)/shard_map/ppermute | solution.py:241
  91.1 6.3 %collective-permute-start.16 = (f32[264,128]{1,0:T(8,128)S(1)}, f32[264,128]{1,0:T(8,128)S(1)}, u32[]{:S(2)}, u32[]{:S(2)}) collective-permute-start(f32[264,128]{1,0:T(8,128)S(1)} %get-tuple-element.54), channel_id=1, source_target_pairs={{0,192},{16,208},{32,224},{48,240},{64,128},{80,144},{96,160},{112... | collective-permute-start | bytes 405512 | tf_op jit(solution)/shard_map/ppermute | solution.py:215
  93.2 6.5 %collective-permute-start.15 = (f32[264,128]{1,0:T(8,128)S(1)}, f32[264,128]{1,0:T(8,128)S(1)}, u32[]{:S(2)}, u32[]{:S(2)}) collective-permute-start(f32[264,128]{1,0:T(8,128)S(1)} %get-tuple-element.54), channel_id=1, source_target_pairs={{0,128},{16,144},{32,160},{48,176},{64,192},{80,208},{96,224},{112... | collective-permute-start | bytes 405512 | tf_op jit(solution)/shard_map/ppermute | solution.py:215
  99.8 10.3 %collective-permute-start.19 = (f32[264,128]{1,0:T(8,128)S(1)}, f32[264,128]{1,0:T(8,128)S(1)}, u32[]{:S(2)}, u32[]{:S(2)}) collective-permute-start(f32[264,128]{1,0:T(8,128)S(1)} %add_add_fusion.5), channel_id=1, source_target_pairs={{0,48},{16,32},{32,16},{48,0},{64,112},{80,96},{96,80},{112,64},{1... | collective-permute-start | bytes 405512 | tf_op jit(solution)/shard_map/ppermute | solution.py:215
  104.6 6.9 %collective-permute-start.18 = (f32[264,128]{1,0:T(8,128)S(1)}, f32[264,128]{1,0:T(8,128)S(1)}, u32[]{:S(2)}, u32[]{:S(2)}) collective-permute-start(f32[264,128]{1,0:T(8,128)S(1)} %add_add_fusion.5), channel_id=1, source_target_pairs={{0,32},{16,48},{32,0},{48,16},{64,96},{80,112},{96,64},{112,80},{1... | collective-permute-start | bytes 405512 | tf_op jit(solution)/shard_map/ppermute | solution.py:215
  105.1 7.1 %collective-permute-start.17 = (f32[264,128]{1,0:T(8,128)S(1)}, f32[264,128]{1,0:T(8,128)S(1)}, u32[]{:S(2)}, u32[]{:S(2)}) collective-permute-start(f32[264,128]{1,0:T(8,128)S(1)} %add_add_fusion.5), channel_id=1, source_target_pairs={{0,16},{16,0},{32,48},{48,32},{64,80},{80,64},{96,112},{112,96},{1... | collective-permute-start | bytes 405512 | tf_op jit(solution)/shard_map/ppermute | solution.py:215
  115.0 16.7 %collective-permute-start.20 = (f32[4,64,512]{2,1,0:T(8,128)S(1)}, f32[4,64,512]{2,1,0:T(8,128)S(1)}, u32[]{:S(2)}, u32[]{:S(2)}) collective-permute-start(f32[4,64,512]{2,1,0:T(8,128)S(1)} %get-tuple-element.58), channel_id=1, source_target_pairs={{0,1},{1,2},{2,3},{3,4},{4,5},{5,6},{6,7},{7,8},{8,9},{9,10},{10,1... | collective-permute-start | bytes 1572872 | tf_op jit(solution)/shard_map/ppermute | solution.py:241
  135.1 6.5 %collective-permute-start.22 = (f32[264,128]{1,0:T(8,128)S(1)}, f32[264,128]{1,0:T(8,128)S(1)}, u32[]{:S(2)}, u32[]{:S(2)}) collective-permute-start(f32[264,128]{1,0:T(8,128)S(1)} %get-tuple-element.61), channel_id=1, source_target_pairs={{0,128},{16,144},{32,160},{48,176},{64,192},{80,208},{96,224},{112... | collective-permute-start | bytes 405512 | tf_op jit(solution)/shard_map/ppermute | solution.py:215
  142.6 10.1 %collective-permute-start.25 = (f32[264,128]{1,0:T(8,128)S(1)}, f32[264,128]{1,0:T(8,128)S(1)}, u32[]{:S(2)}, u32[]{:S(2)}) collective-permute-start(f32[264,128]{1,0:T(8,128)S(1)} %add_add_fusion.3), channel_id=1, source_target_pairs={{0,32},{16,48},{32,0},{48,16},{64,96},{80,112},{96,64},{112,80},{1... | collective-permute-start | bytes 405512 | tf_op jit(solution)/shard_map/ppermute | solution.py:215
  156.5 19.8 %collective-permute-start.27 = (f32[4,64,512]{2,1,0:T(8,128)S(1)}, f32[4,64,512]{2,1,0:T(8,128)S(1)}, u32[]{:S(2)}, u32[]{:S(2)}) collective-permute-start(f32[4,64,512]{2,1,0:T(8,128)S(1)} %get-tuple-element.65), channel_id=1, source_target_pairs={{0,1},{1,2},{2,3},{3,4},{4,5},{5,6},{6,7},{7,8},{8,9},{9,10},{10,1... | collective-permute-start | bytes 1572872 | tf_op jit(solution)/shard_map/ppermute | solution.py:241
  179.6 6.5 %collective-permute-start.29 = (f32[264,128]{1,0:T(8,128)S(1)}, f32[264,128]{1,0:T(8,128)S(1)}, u32[]{:S(2)}, u32[]{:S(2)}) collective-permute-start(f32[264,128]{1,0:T(8,128)S(1)} %get-tuple-element.68), channel_id=1, source_target_pairs={{0,128},{16,144},{32,160},{48,176},{64,192},{80,208},{96,224},{112... | collective-permute-start | bytes 405512 | tf_op jit(solution)/shard_map/ppermute | solution.py:215
  186.3 8.0 %collective-permute-start.33 = (f32[264,128]{1,0:T(8,128)S(1)}, f32[264,128]{1,0:T(8,128)S(1)}, u32[]{:S(2)}, u32[]{:S(2)}) collective-permute-start(f32[264,128]{1,0:T(8,128)S(1)} %add_add_fusion.1), channel_id=1, source_target_pairs={{0,48},{16,32},{32,16},{48,0},{64,112},{80,96},{96,80},{112,64},{1... | collective-permute-start | bytes 405512 | tf_op jit(solution)/shard_map/ppermute | solution.py:215
  187.5 7.1 %collective-permute-start.32 = (f32[264,128]{1,0:T(8,128)S(1)}, f32[264,128]{1,0:T(8,128)S(1)}, u32[]{:S(2)}, u32[]{:S(2)}) collective-permute-start(f32[264,128]{1,0:T(8,128)S(1)} %add_add_fusion.1), channel_id=1, source_target_pairs={{0,32},{16,48},{32,0},{48,16},{64,96},{80,112},{96,64},{112,80},{1... | collective-permute-start | bytes 405512 | tf_op jit(solution)/shard_map/ppermute | solution.py:215
  198.4 20.4 %collective-permute-start.34 = (f32[4,64,512]{2,1,0:T(8,128)S(1)}, f32[4,64,512]{2,1,0:T(8,128)S(1)}, u32[]{:S(2)}, u32[]{:S(2)}) collective-permute-start(f32[4,64,512]{2,1,0:T(8,128)S(1)} %get-tuple-element.70), channel_id=1, source_target_pairs={{0,1},{1,2},{2,3},{3,4},{4,5},{5,6},{6,7},{7,8},{8,9},{9,10},{10,1... | collective-permute-start | bytes 1572872 | tf_op jit(solution)/shard_map/ppermute | solution.py:241
  (13 other events, 67.7 us)

commit v2 on v1

--- a/solution.py
+++ b/solution.py
@@ -146,15 +146,17 @@
             ymats = [folded(left_form(y), right_form(p)) for y, p in zip(ymats, prods)]
             zmats = prods
             continue
+        ylefts, zlefts = [left_form(y) for y in ymats], [left_form(z) for z in zmats]
         prods = [
-            1.5 * eye - 0.5 * folded(left_form(z), right_form(y)) for z, y in zip(zmats, ymats)
+            1.5 * eye - 0.5 * folded(z, jnp.concatenate([y, y], axis=0))
+            for z, y in zip(zlefts, ylefts)
         ]
         if step == NS_STEPS - 1:
-            zmats = [folded(left_form(z), right_form(p)) for z, p in zip(zmats, prods)]
+            zmats = [folded(z, right_form(p)) for z, p in zip(zlefts, prods)]
         else:
             news = [
-                folded(left_form(jnp.concatenate([y, z], axis=0)), right_form(p))
-                for y, z, p in zip(ymats, zmats, prods)
+                folded(jnp.concatenate([y, z], axis=0), right_form(p))
+                for y, z, p in zip(ylefts, zlefts, prods)
             ]
             ymats = [new[:WIDE] for new in news]
             zmats = [new[WIDE:] for new in news]

time: 221 us -> 221 us (level)
  no operation moved by 1% of the time
where the time goes in v2:
time: 221 us; the launch traced here: 220 us
  waiting for transfers between devices  147 us (67%)
  starting transfers between devices  47.5 us (21%)
  Pallas kernels  23.3 us (11%)
    ppermute x5, waiting for transfers between devices, body(): arrived = lax.ppermute(move, 'pairs', along)  92 us
    ppermute x30, waiting for transfers between devices, from_four(): lax.ppermute(value, 'rows', [(r, other(r, d)) for r in rows])  54.9 us
    ppermute x30, starting transfers between devices, from_four(): lax.ppermute(value, 'rows', [(r, other(r, d)) for r in rows])  47.1 us
    pallas_call x16, Pallas kernels, call(): pl.pallas_call(kernel, out_shape=shapes, in_specs=[SMEM if x.dtype == jnp...  23.3 us
  transfers between devices with their start and end apart: 35, of which 28 were waited for; matrix products, arithmetic and copies ran while one was open for 0% of the time, Pallas kernels for 1%

profile of v2, /device:TPU:64, one launch (start us, length us, event | category | flops | bytes accessed | tf_op | source)
XLA Modules:
  0.0 220.1 jit_solution(3133373482346006745)
XLA Ops:
  3.4 3.1 %collective-permute-start.2 = (f32[264,128]{1,0:T(8,128)S(1)}, f32[264,128]{1,0:T(8,128)S(1)}, u32[]{:S(2)}, u32[]{:S(2)}) collective-permute-start(f32[264,128]{1,0:T(8,128)S(1)} %get-tuple-element.40), channel_id=1, source_target_pairs={{0,192},{16,208},{32,224},{48,240},{64,128},{80,144},{96,160},{112... | collective-permute-start | bytes 405512 | tf_op jit(solution)/shard_map/ppermute | solution.py:217
  7.6 4.7 %collective-permute-done.2 = f32[264,128]{1,0:T(8,128)S(1)} collective-permute-done((f32[264,128]{1,0:T(8,128)S(1)}, f32[264,128]{1,0:T(8,128)S(1)}, u32[]{:S(2)}, u32[]{:S(2)}) %collective-permute-start.2) | collective-permute-done | bytes 135200 | tf_op jit(solution)/shard_map/ppermute | solution.py:217
  14.8 4.2 %collective-permute-start.4 = (f32[264,128]{1,0:T(8,128)S(1)}, f32[264,128]{1,0:T(8,128)S(1)}, u32[]{:S(2)}, u32[]{:S(2)}) collective-permute-start(f32[264,128]{1,0:T(8,128)S(1)} %add_add_fusion.9), channel_id=1, source_target_pairs={{0,32},{16,48},{32,0},{48,16},{64,96},{80,112},{96,64},{112,80},{1... | collective-permute-start | bytes 405512 | tf_op jit(solution)/shard_map/ppermute | solution.py:217
  18.9 6.5 %collective-permute-done.5 = f32[264,128]{1,0:T(8,128)S(1)} collective-permute-done((f32[264,128]{1,0:T(8,128)S(1)}, f32[264,128]{1,0:T(8,128)S(1)}, u32[]{:S(2)}, u32[]{:S(2)}) %collective-permute-start.5) | collective-permute-done | bytes 135200 | tf_op jit(solution)/shard_map/ppermute | solution.py:217
  25.5 2.7 %shard_map.29 = (f32[4,64,512]{2,1,0:T(8,128)S(1)}, f32[4,64,128]{2,1,0:T(8,128)S(1)}) custom-call(bf16[8,64,512]{2,1,0:T(8,128)(2,1)S(1)} %get-tuple-element.38.high_ref, bf16[8,64,512]{2,1,0:T(8,128)(2,1)S(1)} %get-tuple-element.39.low_ref, f32[264,128]{1,0:T(8,128)S(1)} %add_add_fusion.8.sums_ref), custom_call_target="tpu_custom_call" | custom-call | tf_op jit(solution)/shard_map/pallas_call | solution.py:196
  28.7 19.8 %collective-permute-done.6.arrived_ref = f32[4,64,512]{2,1,0:T(8,128)S(1)} collective-permute-done((f32[4,64,512]{2,1,0:T(8,128)S(1)}, f32[4,64,512]{2,1,0:T(8,128)S(1)}, u32[]{:S(2)}, u32[]{:S(2)}) %collective-permute-start.6) | collective-permute-done | bytes 524320 | tf_op jit(solution)/shard_map/ppermute | solution.py:243
  49.7 3.0 %collective-permute-start.9 = (f32[264,128]{1,0:T(8,128)S(1)}, f32[264,128]{1,0:T(8,128)S(1)}, u32[]{:S(2)}, u32[]{:S(2)}) collective-permute-start(f32[264,128]{1,0:T(8,128)S(1)} %get-tuple-element.47), channel_id=1, source_target_pairs={{0,192},{16,208},{32,224},{48,240},{64,128},{80,144},{96,160},{112... | collective-permute-start | bytes 405512 | tf_op jit(solution)/shard_map/ppermute | solution.py:217
  53.9 2.9 %collective-permute-done.9 = f32[264,128]{1,0:T(8,128)S(1)} collective-permute-done((f32[264,128]{1,0:T(8,128)S(1)}, f32[264,128]{1,0:T(8,128)S(1)}, u32[]{:S(2)}, u32[]{:S(2)}) %collective-permute-start.9) | collective-permute-done | bytes 135200 | tf_op jit(solution)/shard_map/ppermute | solution.py:217
  56.8 2.5 %collective-permute-done.8 = f32[264,128]{1,0:T(8,128)S(1)} collective-permute-done((f32[264,128]{1,0:T(8,128)S(1)}, f32[264,128]{1,0:T(8,128)S(1)}, u32[]{:S(2)}, u32[]{:S(2)}) %collective-permute-start.8) | collective-permute-done | bytes 135200 | tf_op jit(solution)/shard_map/ppermute | solution.py:217
  60.1 4.9 %collective-permute-start.11 = (f32[264,128]{1,0:T(8,128)S(1)}, f32[264,128]{1,0:T(8,128)S(1)}, u32[]{:S(2)}, u32[]{:S(2)}) collective-permute-start(f32[264,128]{1,0:T(8,128)S(1)} %add_add_fusion.7), channel_id=1, source_target_pairs={{0,32},{16,48},{32,0},{48,16},{64,96},{80,112},{96,64},{112,80},{1... | collective-permute-start | bytes 405512 | tf_op jit(solution)/shard_map/ppermute | solution.py:217
  65.3 4.2 %collective-permute-done.11 = f32[264,128]{1,0:T(8,128)S(1)} collective-permute-done((f32[264,128]{1,0:T(8,128)S(1)}, f32[264,128]{1,0:T(8,128)S(1)}, u32[]{:S(2)}, u32[]{:S(2)}) %collective-permute-start.11) | collective-permute-done | bytes 135200 | tf_op jit(solution)/shard_map/ppermute | solution.py:217
  70.0 2.7 %shard_map.32 = (f32[4,64,512]{2,1,0:T(8,128)S(1)}, f32[4,64,128]{2,1,0:T(8,128)S(1)}) custom-call(bf16[8,64,512]{2,1,0:T(8,128)(2,1)S(1)} %get-tuple-element.45.high_ref, bf16[8,64,512]{2,1,0:T(8,128)(2,1)S(1)} %get-tuple-element.46.low_ref, f32[264,128]{1,0:T(8,128)S(1)} %add_add_fusion.6.sums_ref), custom_call_target="tpu_custom_call" | custom-call | tf_op jit(solution)/shard_map/pallas_call | solution.py:196
  73.2 16.6 %collective-permute-done.13.arrived_ref = f32[4,64,512]{2,1,0:T(8,128)S(1)} collective-permute-done((f32[4,64,512]{2,1,0:T(8,128)S(1)}, f32[4,64,512]{2,1,0:T(8,128)S(1)}, u32[]{:S(2)}, u32[]{:S(2)}) %collective-permute-start.13) | collective-permute-done | bytes 524320 | tf_op jit(solution)/shard_map/ppermute | solution.py:243
  99.8 4.8 %collective-permute-start.19 = (f32[264,128]{1,0:T(8,128)S(1)}, f32[264,128]{1,0:T(8,128)S(1)}, u32[]{:S(2)}, u32[]{:S(2)}) collective-permute-start(f32[264,128]{1,0:T(8,128)S(1)} %add_add_fusion.5), channel_id=1, source_target_pairs={{0,48},{16,32},{32,16},{48,0},{64,112},{80,96},{96,80},{112,64},{1... | collective-permute-start | bytes 405512 | tf_op jit(solution)/shard_map/ppermute | solution.py:217
  106.3 3.8 %collective-permute-done.19 = f32[264,128]{1,0:T(8,128)S(1)} collective-permute-done((f32[264,128]{1,0:T(8,128)S(1)}, f32[264,128]{1,0:T(8,128)S(1)}, u32[]{:S(2)}, u32[]{:S(2)}) %collective-permute-start.19) | collective-permute-done | bytes 135200 | tf_op jit(solution)/shard_map/ppermute | solution.py:217
  112.2 2.7 %shard_map.35 = (f32[4,64,512]{2,1,0:T(8,128)S(1)}, f32[4,64,128]{2,1,0:T(8,128)S(1)}) custom-call(bf16[8,64,512]{2,1,0:T(8,128)(2,1)S(1)} %get-tuple-element.52.high_ref, bf16[8,64,512]{2,1,0:T(8,128)(2,1)S(1)} %get-tuple-element.53.low_ref, f32[264,128]{1,0:T(8,128)S(1)} %add_add_fusion.4.sums_ref), custom_call_target="tpu_custom_call" | custom-call | tf_op jit(solution)/shard_map/pallas_call | solution.py:196
  115.4 16.3 %collective-permute-done.20.arrived_ref = f32[4,64,512]{2,1,0:T(8,128)S(1)} collective-permute-done((f32[4,64,512]{2,1,0:T(8,128)S(1)}, f32[4,64,512]{2,1,0:T(8,128)S(1)}, u32[]{:S(2)}, u32[]{:S(2)}) %collective-permute-start.20) | collective-permute-done | bytes 524320 | tf_op jit(solution)/shard_map/ppermute | solution.py:243
  142.6 5.0 %collective-permute-start.25 = (f32[264,128]{1,0:T(8,128)S(1)}, f32[264,128]{1,0:T(8,128)S(1)}, u32[]{:S(2)}, u32[]{:S(2)}) collective-permute-start(f32[264,128]{1,0:T(8,128)S(1)} %add_add_fusion.3), channel_id=1, source_target_pairs={{0,32},{16,48},{32,0},{48,16},{64,96},{80,112},{96,64},{112,80},{1... | collective-permute-start | bytes 405512 | tf_op jit(solution)/shard_map/ppermute | solution.py:217
  147.8 4.9 %collective-permute-done.25 = f32[264,128]{1,0:T(8,128)S(1)} collective-permute-done((f32[264,128]{1,0:T(8,128)S(1)}, f32[264,128]{1,0:T(8,128)S(1)}, u32[]{:S(2)}, u32[]{:S(2)}) %collective-permute-start.25) | collective-permute-done | bytes 135200 | tf_op jit(solution)/shard_map/ppermute | solution.py:217
  153.8 2.7 %shard_map.38 = (f32[4,64,512]{2,1,0:T(8,128)S(1)}, f32[4,64,128]{2,1,0:T(8,128)S(1)}) custom-call(bf16[8,64,512]{2,1,0:T(8,128)(2,1)S(1)} %get-tuple-element.59.high_ref, bf16[8,64,512]{2,1,0:T(8,128)(2,1)S(1)} %get-tuple-element.60.low_ref, f32[264,128]{1,0:T(8,128)S(1)} %add_add_fusion.2.sums_ref), custom_call_target="tpu_custom_call" | custom-call | tf_op jit(solution)/shard_map/pallas_call | solution.py:196
  156.9 19.4 %collective-permute-done.27.arrived_ref = f32[4,64,512]{2,1,0:T(8,128)S(1)} collective-permute-done((f32[4,64,512]{2,1,0:T(8,128)S(1)}, f32[4,64,512]{2,1,0:T(8,128)S(1)}, u32[]{:S(2)}, u32[]{:S(2)}) %collective-permute-start.27) | collective-permute-done | bytes 524320 | tf_op jit(solution)/shard_map/ppermute | solution.py:243
  189.8 4.4 %collective-permute-done.33 = f32[264,128]{1,0:T(8,128)S(1)} collective-permute-done((f32[264,128]{1,0:T(8,128)S(1)}, f32[264,128]{1,0:T(8,128)S(1)}, u32[]{:S(2)}, u32[]{:S(2)}) %collective-permute-start.33) | collective-permute-done | bytes 135200 | tf_op jit(solution)/shard_map/ppermute | solution.py:217
  195.7 2.7 %shard_map.41 = (f32[4,64,512]{2,1,0:T(8,128)S(1)}, f32[4,64,128]{2,1,0:T(8,128)S(1)}) custom-call(bf16[8,64,512]{2,1,0:T(8,128)(2,1)S(1)} %get-tuple-element.66.high_ref, bf16[8,64,512]{2,1,0:T(8,128)(2,1)S(1)} %get-tuple-element.67.low_ref, f32[264,128]{1,0:T(8,128)S(1)} %add_add_fusion.sums_ref), custom_call_target="tpu_custom_call" | custom-call | tf_op jit(solution)/shard_map/pallas_call | solution.py:196
  198.8 19.9 %collective-permute-done.34.arrived_ref = f32[4,64,512]{2,1,0:T(8,128)S(1)} collective-permute-done((f32[4,64,512]{2,1,0:T(8,128)S(1)}, f32[4,64,512]{2,1,0:T(8,128)S(1)}, u32[]{:S(2)}, u32[]{:S(2)}) %collective-permute-start.34) | collective-permute-done | bytes 524320 | tf_op jit(solution)/shard_map/ppermute | solution.py:243
  (76 shorter events, 55.4 us)
Async XLA Ops:
  3.4 8.9 %collective-permute-start.2 = (f32[264,128]{1,0:T(8,128)S(1)}, f32[264,128]{1,0:T(8,128)S(1)}, u32[]{:S(2)}, u32[]{:S(2)}) collective-permute-start(f32[264,128]{1,0:T(8,128)S(1)} %get-tuple-element.40), channel_id=1, source_target_pairs={{0,192},{16,208},{32,224},{48,240},{64,128},{80,144},{96,160},{112... | collective-permute-start | bytes 405512 | tf_op jit(solution)/shard_map/ppermute | solution.py:217
  6.5 8.0 %collective-permute-start.1 = (f32[264,128]{1,0:T(8,128)S(1)}, f32[264,128]{1,0:T(8,128)S(1)}, u32[]{:S(2)}, u32[]{:S(2)}) collective-permute-start(f32[264,128]{1,0:T(8,128)S(1)} %get-tuple-element.40), channel_id=1, source_target_pairs={{0,128},{16,144},{32,160},{48,176},{64,192},{80,208},{96,224},{112... | collective-permute-start | bytes 405512 | tf_op jit(solution)/shard_map/ppermute | solution.py:217
  7.2 7.4 %collective-permute-start = (f32[264,128]{1,0:T(8,128)S(1)}, f32[264,128]{1,0:T(8,128)S(1)}, u32[]{:S(2)}, u32[]{:S(2)}) collective-permute-start(f32[264,128]{1,0:T(8,128)S(1)} %get-tuple-element.40), channel_id=1, source_target_pairs={{0,64},{16,80},{32,96},{48,112},{64,0},{80,16},{96,32},{112,48},{1... | collective-permute-start | bytes 405512 | tf_op jit(solution)/shard_map/ppermute | solution.py:217
  14.6 10.9 %collective-permute-start.5 = (f32[264,128]{1,0:T(8,128)S(1)}, f32[264,128]{1,0:T(8,128)S(1)}, u32[]{:S(2)}, u32[]{:S(2)}) collective-permute-start(f32[264,128]{1,0:T(8,128)S(1)} %add_add_fusion.9), channel_id=1, source_target_pairs={{0,48},{16,32},{32,16},{48,0},{64,112},{80,96},{96,80},{112,64},{1... | collective-permute-start | bytes 405512 | tf_op jit(solution)/shard_map/ppermute | solution.py:217
  14.8 10.7 %collective-permute-start.4 = (f32[264,128]{1,0:T(8,128)S(1)}, f32[264,128]{1,0:T(8,128)S(1)}, u32[]{:S(2)}, u32[]{:S(2)}) collective-permute-start(f32[264,128]{1,0:T(8,128)S(1)} %add_add_fusion.9), channel_id=1, source_target_pairs={{0,32},{16,48},{32,0},{48,16},{64,96},{80,112},{96,64},{112,80},{1... | collective-permute-start | bytes 405512 | tf_op jit(solution)/shard_map/ppermute | solution.py:217
  18.9 6.5 %collective-permute-start.3 = (f32[264,128]{1,0:T(8,128)S(1)}, f32[264,128]{1,0:T(8,128)S(1)}, u32[]{:S(2)}, u32[]{:S(2)}) collective-permute-start(f32[264,128]{1,0:T(8,128)S(1)} %add_add_fusion.9), channel_id=1, source_target_pairs={{0,16},{16,0},{32,48},{48,32},{64,80},{80,64},{96,112},{112,96},{1... | collective-permute-start | bytes 405512 | tf_op jit(solution)/shard_map/ppermute | solution.py:217
  28.3 20.2 %collective-permute-start.6 = (f32[4,64,512]{2,1,0:T(8,128)S(1)}, f32[4,64,512]{2,1,0:T(8,128)S(1)}, u32[]{:S(2)}, u32[]{:S(2)}) collective-permute-start(f32[4,64,512]{2,1,0:T(8,128)S(1)} %get-tuple-element.44), channel_id=1, source_target_pairs={{0,1},{1,2},{2,3},{3,4},{4,5},{5,6},{6,7},{7,8},{8,9},{9,10},{10,1... | collective-permute-start | bytes 1572872 | tf_op jit(solution)/shard_map/ppermute | solution.py:243
  49.7 7.1 %collective-permute-start.9 = (f32[264,128]{1,0:T(8,128)S(1)}, f32[264,128]{1,0:T(8,128)S(1)}, u32[]{:S(2)}, u32[]{:S(2)}) collective-permute-start(f32[264,128]{1,0:T(8,128)S(1)} %get-tuple-element.47), channel_id=1, source_target_pairs={{0,192},{16,208},{32,224},{48,240},{64,128},{80,144},{96,160},{112... | collective-permute-start | bytes 405512 | tf_op jit(solution)/shard_map/ppermute | solution.py:217
  52.8 6.5 %collective-permute-start.8 = (f32[264,128]{1,0:T(8,128)S(1)}, f32[264,128]{1,0:T(8,128)S(1)}, u32[]{:S(2)}, u32[]{:S(2)}) collective-permute-start(f32[264,128]{1,0:T(8,128)S(1)} %get-tuple-element.47), channel_id=1, source_target_pairs={{0,128},{16,144},{32,160},{48,176},{64,192},{80,208},{96,224},{112... | collective-permute-start | bytes 405512 | tf_op jit(solution)/shard_map/ppermute | solution.py:217
  60.1 9.4 %collective-permute-start.11 = (f32[264,128]{1,0:T(8,128)S(1)}, f32[264,128]{1,0:T(8,128)S(1)}, u32[]{:S(2)}, u32[]{:S(2)}) collective-permute-start(f32[264,128]{1,0:T(8,128)S(1)} %add_add_fusion.7), channel_id=1, source_target_pairs={{0,32},{16,48},{32,0},{48,16},{64,96},{80,112},{96,64},{112,80},{1... | collective-permute-start | bytes 405512 | tf_op jit(solution)/shard_map/ppermute | solution.py:217
  72.7 17.0 %collective-permute-start.13 = (f32[4,64,512]{2,1,0:T(8,128)S(1)}, f32[4,64,512]{2,1,0:T(8,128)S(1)}, u32[]{:S(2)}, u32[]{:S(2)}) collective-permute-start(f32[4,64,512]{2,1,0:T(8,128)S(1)} %get-tuple-element.51), channel_id=1, source_target_pairs={{0,1},{1,2},{2,3},{3,4},{4,5},{5,6},{6,7},{7,8},{8,9},{9,10},{10,1... | collective-permute-start | bytes 1572872 | tf_op jit(solution)/shard_map/ppermute | solution.py:243
  91.1 6.3 %collective-permute-start.16 = (f32[264,128]{1,0:T(8,128)S(1)}, f32[264,128]{1,0:T(8,128)S(1)}, u32[]{:S(2)}, u32[]{:S(2)}) collective-permute-start(f32[264,128]{1,0:T(8,128)S(1)} %get-tuple-element.54), channel_id=1, source_target_pairs={{0,192},{16,208},{32,224},{48,240},{64,128},{80,144},{96,160},{112... | collective-permute-start | bytes 405512 | tf_op jit(solution)/shard_map/ppermute | solution.py:217
  93.2 6.5 %collective-permute-start.15 = (f32[264,128]{1,0:T(8,128)S(1)}, f32[264,128]{1,0:T(8,128)S(1)}, u32[]{:S(2)}, u32[]{:S(2)}) collective-permute-start(f32[264,128]{1,0:T(8,128)S(1)} %get-tuple-element.54), channel_id=1, source_target_pairs={{0,128},{16,144},{32,160},{48,176},{64,192},{80,208},{96,224},{112... | collective-permute-start | bytes 405512 | tf_op jit(solution)/shard_map/ppermute | solution.py:217
  99.8 10.3 %collective-permute-start.19 = (f32[264,128]{1,0:T(8,128)S(1)}, f32[264,128]{1,0:T(8,128)S(1)}, u32[]{:S(2)}, u32[]{:S(2)}) collective-permute-start(f32[264,128]{1,0:T(8,128)S(1)} %add_add_fusion.5), channel_id=1, source_target_pairs={{0,48},{16,32},{32,16},{48,0},{64,112},{80,96},{96,80},{112,64},{1... | collective-permute-start | bytes 405512 | tf_op jit(solution)/shard_map/ppermute | solution.py:217
  104.6 6.9 %collective-permute-start.18 = (f32[264,128]{1,0:T(8,128)S(1)}, f32[264,128]{1,0:T(8,128)S(1)}, u32[]{:S(2)}, u32[]{:S(2)}) collective-permute-start(f32[264,128]{1,0:T(8,128)S(1)} %add_add_fusion.5), channel_id=1, source_target_pairs={{0,32},{16,48},{32,0},{48,16},{64,96},{80,112},{96,64},{112,80},{1... | collective-permute-start | bytes 405512 | tf_op jit(solution)/shard_map/ppermute | solution.py:217
  105.1 7.1 %collective-permute-start.17 = (f32[264,128]{1,0:T(8,128)S(1)}, f32[264,128]{1,0:T(8,128)S(1)}, u32[]{:S(2)}, u32[]{:S(2)}) collective-permute-start(f32[264,128]{1,0:T(8,128)S(1)} %add_add_fusion.5), channel_id=1, source_target_pairs={{0,16},{16,0},{32,48},{48,32},{64,80},{80,64},{96,112},{112,96},{1... | collective-permute-start | bytes 405512 | tf_op jit(solution)/shard_map/ppermute | solution.py:217
  115.0 16.7 %collective-permute-start.20 = (f32[4,64,512]{2,1,0:T(8,128)S(1)}, f32[4,64,512]{2,1,0:T(8,128)S(1)}, u32[]{:S(2)}, u32[]{:S(2)}) collective-permute-start(f32[4,64,512]{2,1,0:T(8,128)S(1)} %get-tuple-element.58), channel_id=1, source_target_pairs={{0,1},{1,2},{2,3},{3,4},{4,5},{5,6},{6,7},{7,8},{8,9},{9,10},{10,1... | collective-permute-start | bytes 1572872 | tf_op jit(solution)/shard_map/ppermute | solution.py:243
  135.1 6.5 %collective-permute-start.22 = (f32[264,128]{1,0:T(8,128)S(1)}, f32[264,128]{1,0:T(8,128)S(1)}, u32[]{:S(2)}, u32[]{:S(2)}) collective-permute-start(f32[264,128]{1,0:T(8,128)S(1)} %get-tuple-element.61), channel_id=1, source_target_pairs={{0,128},{16,144},{32,160},{48,176},{64,192},{80,208},{96,224},{112... | collective-permute-start | bytes 405512 | tf_op jit(solution)/shard_map/ppermute | solution.py:217
  142.6 10.1 %collective-permute-start.25 = (f32[264,128]{1,0:T(8,128)S(1)}, f32[264,128]{1,0:T(8,128)S(1)}, u32[]{:S(2)}, u32[]{:S(2)}) collective-permute-start(f32[264,128]{1,0:T(8,128)S(1)} %add_add_fusion.3), channel_id=1, source_target_pairs={{0,32},{16,48},{32,0},{48,16},{64,96},{80,112},{96,64},{112,80},{1... | collective-permute-start | bytes 405512 | tf_op jit(solution)/shard_map/ppermute | solution.py:217
  156.5 19.8 %collective-permute-start.27 = (f32[4,64,512]{2,1,0:T(8,128)S(1)}, f32[4,64,512]{2,1,0:T(8,128)S(1)}, u32[]{:S(2)}, u32[]{:S(2)}) collective-permute-start(f32[4,64,512]{2,1,0:T(8,128)S(1)} %get-tuple-element.65), channel_id=1, source_target_pairs={{0,1},{1,2},{2,3},{3,4},{4,5},{5,6},{6,7},{7,8},{8,9},{9,10},{10,1... | collective-permute-start | bytes 1572872 | tf_op jit(solution)/shard_map/ppermute | solution.py:243
  179.6 6.5 %collective-permute-start.29 = (f32[264,128]{1,0:T(8,128)S(1)}, f32[264,128]{1,0:T(8,128)S(1)}, u32[]{:S(2)}, u32[]{:S(2)}) collective-permute-start(f32[264,128]{1,0:T(8,128)S(1)} %get-tuple-element.68), channel_id=1, source_target_pairs={{0,128},{16,144},{32,160},{48,176},{64,192},{80,208},{96,224},{112... | collective-permute-start | bytes 405512 | tf_op jit(solution)/shard_map/ppermute | solution.py:217
  186.3 8.0 %collective-permute-start.33 = (f32[264,128]{1,0:T(8,128)S(1)}, f32[264,128]{1,0:T(8,128)S(1)}, u32[]{:S(2)}, u32[]{:S(2)}) collective-permute-start(f32[264,128]{1,0:T(8,128)S(1)} %add_add_fusion.1), channel_id=1, source_target_pairs={{0,48},{16,32},{32,16},{48,0},{64,112},{80,96},{96,80},{112,64},{1... | collective-permute-start | bytes 405512 | tf_op jit(solution)/shard_map/ppermute | solution.py:217
  187.4 7.1 %collective-permute-start.32 = (f32[264,128]{1,0:T(8,128)S(1)}, f32[264,128]{1,0:T(8,128)S(1)}, u32[]{:S(2)}, u32[]{:S(2)}) collective-permute-start(f32[264,128]{1,0:T(8,128)S(1)} %add_add_fusion.1), channel_id=1, source_target_pairs={{0,32},{16,48},{32,0},{48,16},{64,96},{80,112},{96,64},{112,80},{1... | collective-permute-start | bytes 405512 | tf_op jit(solution)/shard_map/ppermute | solution.py:217
  198.4 20.4 %collective-permute-start.34 = (f32[4,64,512]{2,1,0:T(8,128)S(1)}, f32[4,64,512]{2,1,0:T(8,128)S(1)}, u32[]{:S(2)}, u32[]{:S(2)}) collective-permute-start(f32[4,64,512]{2,1,0:T(8,128)S(1)} %get-tuple-element.70), channel_id=1, source_target_pairs={{0,1},{1,2},{2,3},{3,4},{4,5},{5,6},{6,7},{7,8},{8,9},{9,10},{10,1... | collective-permute-start | bytes 1572872 | tf_op jit(solution)/shard_map/ppermute | solution.py:243
  (13 other events, 67.7 us)
